TPU v7x, 256 devices: a whole 4x4x8 slice. The times are simulated.
256 devices in a mesh: gx: 32 (over x, z), gy: 8 (over y, core).
Axes of the slice: x: 4, y: 4, z: 8, core: 2. Of those that a mesh axis runs over, the one named last changes fastest.
Arguments:
- ensemble: float32 [64, 2048, 2048], P('gx', None, 'gy'), may hold values from -6 to 6
- obs_values: float32 [4, 128], replicated, may hold values from -6 to 6
- obs_error: float32 [4, 128], replicated, may hold values from 0.3 to 3
- tile_weight: float32 [4, 128, 32, 8], P(None, None, 'gx', 'gy'), may hold values from 0.2 to 1
- owner_device: int32 [4], replicated, may hold values from 0 to 255
- obs_cells: int32 [4, 128], replicated, may hold values from 0 to 16383
Outputs:
- analysis_ensemble: float32 [64, 2048, 2048], P('gx', None, 'gy')
Inputs may be any that keep to these rules, and one draw needn't show every extreme that they name: `owner_device`: device numbers count gy fastest: the device at index i of gx and j of gy is number i times the length of gy plus j. `obs_cells`: cell c of a tile lies c // 256 cells along the first direction and c % 256 along the second from the tile's first cell; cells may repeat.
All inputs are finite; a program needn't handle non-finite values.
Results may differ from a plain program's by a relative error of at most 0.00015.
Values sent between devices are 32-bit elements; how exact they have to be, the bound alone decides.
A program may use at most 64 MiB of HBM per device.

v0:
```python
import math

import jax
import jax.numpy as jnp
from jax import lax
from jax.sharding import PartitionSpec as P

EPSILON = 1e-06
PRECISE = lax.Precision.HIGHEST


def spread_2(shard, axis, root):
    mine = lax.axis_index(axis) == root
    return lax.psum(jnp.where(mine, shard, jnp.zeros_like(shard)), axis)


def analysis(prior_ens, values, errors):
    members = prior_ens.shape[1]
    average = jnp.mean(prior_ens, axis=1, keepdims=True)
    anomaly = prior_ens - average
    spread = jnp.sum(anomaly * anomaly, axis=1, keepdims=True) / (members - 1) + EPSILON
    obs_noise = errors[:, None]
    post_var = 1.0 / (1.0 / spread + 1.0 / obs_noise)
    post_mean = post_var * (average / spread + values[:, None] / obs_noise)
    increment = post_mean - average + (jnp.sqrt(post_var / spread) - 1.0) * anomaly
    return (anomaly, spread, increment)


def regression(
    state_cols,
    anomaly,
    spread,
    increment,
    weight_cols,
    obs_xpos,
    obs_ypos,
    grid_xpos,
    grid_ypos,
    radius,
):
    members = state_cols.shape[0]
    deviation = state_cols - jnp.mean(state_cols, axis=0, keepdims=True)
    covariance = jnp.dot(anomaly, deviation, precision=PRECISE) / (members - 1)
    distance = (grid_xpos[None, :] - obs_xpos[:, None]) ** 2 + (
        grid_ypos[None, :] - obs_ypos[:, None]
    ) ** 2
    tapering = 1.0 / (1.0 + distance / radius)
    gain_rows = covariance * (tapering * weight_cols) / spread
    return state_cols + jnp.dot(increment.T, gain_rows, precision=PRECISE)


def blocked_regression(
    state_cols,
    anomaly,
    spread,
    increment,
    weight_cols,
    obs_xpos,
    obs_ypos,
    grid_xpos,
    grid_ypos,
    radius,
):
    members, cell_count = state_cols.shape
    breadth = math.gcd(cell_count, 512)
    pieces = cell_count // breadth
    stacked = state_cols.reshape(members, pieces, breadth).transpose(1, 0, 2)
    row_coords = grid_xpos.reshape(pieces, breadth)
    col_coords = grid_ypos.reshape(pieces, breadth)

    def update_piece(element):
        states, rows_here, cols_here = element
        return regression(
            states,
            anomaly,
            spread,
            increment,
            weight_cols,
            obs_xpos,
            obs_ypos,
            rows_here,
            cols_here,
            radius,
        )

    updated = lax.map(update_piece, (stacked, row_coords, col_coords))
    return updated.transpose(1, 0, 2).reshape(members, cell_count)


def local(ensemble, obs_values, obs_error, tile_weight, owner_device, obs_cells):
    gx_count = lax.axis_size("gx")
    gy_count = lax.axis_size("gy")
    members = ensemble.shape[0] * gx_count
    tile_rows = ensemble.shape[1] // gx_count
    tile_cols = ensemble.shape[2]
    cell_count = tile_rows * tile_cols
    radius = float((tile_rows * gx_count // 4) ** 2)
    row_index = lax.axis_index("gx")
    col_index = lax.axis_index("gy")
    cell_ids = jnp.arange(cell_count, dtype=jnp.int32)
    grid_xpos = (row_index * tile_rows + cell_ids // tile_cols).astype(jnp.float32)
    grid_ypos = (col_index * tile_cols + cell_ids % tile_cols).astype(jnp.float32)
    batches = obs_cells.shape[0]
    tile_state = lax.all_to_all(ensemble, "gx", split_axis=1, concat_axis=0, tiled=True).reshape(
        members, cell_count
    )
    for batch in range(batches):
        observed = obs_cells[batch]
        own_prior = jnp.take(tile_state, observed, axis=1).T
        root_index = owner_device[batch]
        prior_ens = spread_2(own_prior, ("gx", "gy"), root_index)
        anomaly, spread, increment = analysis(prior_ens, obs_values[batch], obs_error[batch])
        obs_xpos = (root_index // gy_count * tile_rows + observed // tile_cols).astype(jnp.float32)
        obs_ypos = (root_index % gy_count * tile_cols + observed % tile_cols).astype(jnp.float32)
        weight_cols = tile_weight[batch, :, 0, 0][:, None]
        tile_state = blocked_regression(
            tile_state,
            anomaly,
            spread,
            increment,
            weight_cols,
            obs_xpos,
            obs_ypos,
            grid_xpos,
            grid_ypos,
            radius,
        )
    result = lax.all_to_all(
        tile_state.reshape(members, tile_rows, tile_cols),
        "gx",
        split_axis=0,
        concat_axis=1,
        tiled=True,
    )
    return result


def solution(mesh):
    placed = (P("gx", None, "gy"), P(), P(), P(None, None, "gx", "gy"), P(), P())
    return jax.shard_map(
        local, mesh=mesh, in_specs=placed, out_specs=P("gx", None, "gy"), check_vma=False
    )
```

profile of v0, /device:TPU:32, one launch (start us, length us, event | category | flops | bytes accessed | tf_op | source)
XLA Modules:
  0.0 1130.8 jit_solution(357414713133553755)
XLA Ops:
  0.0 8.7 copy.26
  8.7 11.4 %all-to-all-start = ((f32[2,2048,256]{2,0,1:T(2,128)}), f32[2,2048,256]{2,0,1:T(2,128)}, u32[]{:S(2)}, u32[]{:S(2)}) async-start(f32[2,2048,256]{2,0,1:T(2,128)} %copy.26), calls=%async_computation | async-start | bytes 8388608 | tf_op jit(solution)/shard_map/all_to_all | solution.py:104
  33.7 81.9 %all-to-all-done = f32[2,2048,256]{2,0,1:T(2,128)} async-done(((f32[2,2048,256]{2,0,1:T(2,128)}), f32[2,2048,256]{2,0,1:T(2,128)}, u32[]{:S(2)}, u32[]{:S(2)}) %all-to-all-start) | async-done | bytes 4194336 | tf_op jit(solution)/shard_map/all_to_all | solution.py:104
  118.5 4.4 copy.37
  122.8 6.9 copy.28
  129.7 4.0 gather_fusion
  133.9 76.7 %psum.28 = f32[128,64]{1,0:T(8,128)S(1)} all-reduce(f32[128,64]{1,0:T(8,128)S(1)} %fusion.42), channel_id=1, replica_groups=mesh['gx'=32,'gy'=8] {'gx','gy'}, use_global_device_ids=true, to_apply=%region_0.2 | all-reduce | flops 8192 | bytes 65536 | tf_op jit(solution)/shard_map/psum | solution.py:14
  210.9 5.2 reshape_reshape.6
  218.7 101.1 %while.40 = (s32[]{:T(128)}, f32[32,64,512]{2,1,0:T(8,128)}, f32[32,64,512]{2,0,1:T(8,128)}, f32[128,64]{1,0:T(8,128)S(1)}, f32[32,512]{1,0:T(8,128)S(1)}, /*ind...) while((s32[]{:T(128)}, f32[32,64,512]{2,1,0:T(8,128)}, ...), condition=%wide.region_5.7_spmd, body=%wide.region_3.6_spmd.sunk | while | flops 101548032 | bytes 1268349 | solution.py:86
  319.8 6.9 copy.30
  326.7 4.0 gather_fusion.1
  330.8 73.0 %psum.29 = f32[128,64]{1,0:T(8,128)S(1)} all-reduce(f32[128,64]{1,0:T(8,128)S(1)} %fusion.41), channel_id=1, replica_groups=mesh['gx'=32,'gy'=8] {'gx','gy'}, use_global_device_ids=true, to_apply=%region_6.8 | all-reduce | flops 8192 | bytes 65536 | tf_op jit(solution)/shard_map/psum | solution.py:14
  406.8 143.9 %while.41 = (s32[]{:T(128)}, f32[32,64,512]{2,1,0:T(8,128)}, f32[32,64,512]{2,1,0:T(8,128)}, f32[128,64]{1,0:T(8,128)S(1)}, f32[32,512]{1,0:T(8,128)S(1)}, /*ind...) while((s32[]{:T(128)}, f32[32,64,512]{2,1,0:T(8,128)}, ...), condition=%wide.region_11.13_spmd, body=%wide.region_9.12_spmd.sunk | while | flops 101548032 | bytes 1137789 | solution.py:86
  550.7 6.9 copy.31
  557.6 4.0 gather_fusion.2
  561.7 73.6 %psum.30 = f32[128,64]{1,0:T(8,128)S(1)} all-reduce(f32[128,64]{1,0:T(8,128)S(1)} %fusion.40), channel_id=1, replica_groups=mesh['gx'=32,'gy'=8] {'gx','gy'}, use_global_device_ids=true, to_apply=%region_12.14 | all-reduce | flops 8192 | bytes 65536 | tf_op jit(solution)/shard_map/psum | solution.py:14
  638.3 143.6 %while.42 = (s32[]{:T(128)}, f32[32,64,512]{2,1,0:T(8,128)}, f32[32,64,512]{2,1,0:T(8,128)}, f32[128,64]{1,0:T(8,128)S(1)}, f32[32,512]{1,0:T(8,128)S(1)}, /*ind...) while((s32[]{:T(128)}, f32[32,64,512]{2,1,0:T(8,128)}, ...), condition=%wide.region_17.19_spmd, body=%wide.region_15.18_spmd.sunk | while | flops 101548032 | bytes 1137789 | solution.py:86
  781.9 6.9 copy.32
  788.8 4.0 gather_fusion.3
  793.0 74.5 %psum.31 = f32[128,64]{1,0:T(8,128)S(1)} all-reduce(f32[128,64]{1,0:T(8,128)S(1)} %fusion.39), channel_id=1, replica_groups=mesh['gx'=32,'gy'=8] {'gx','gy'}, use_global_device_ids=true, to_apply=%region_18.20 | all-reduce | flops 8192 | bytes 65536 | tf_op jit(solution)/shard_map/psum | solution.py:14
  870.4 143.9 %while.43 = (s32[]{:T(128)}, f32[32,64,512]{2,1,0:T(8,128)}, f32[32,64,512]{2,1,0:T(8,128)}, f32[128,64]{1,0:T(8,128)S(1)}, f32[32,512]{1,0:T(8,128)S(1)}, /*ind...) while((s32[]{:T(128)}, f32[32,64,512]{2,1,0:T(8,128)}, ...), condition=%wide.region_23.25_spmd, body=%wide.region_21.24_spmd.sunk | while | flops 101548032 | bytes 1137789 | solution.py:86
  1014.3 6.5 copy.33
  1020.9 4.9 reshape_reshape.7
  1025.8 102.7 %all_to_all.33 = f32[64,64,256]{2,1,0:T(8,128)S(1)} all-to-all(f32[64,64,256]{2,1,0:T(8,128)} %reshape_reshape.7), channel_id=1, replica_groups=mesh['gx'=32,'gy'=8] {'gx'}, dimensions={0} | all-to-all | bytes 8388608 | tf_op jit(solution)/shard_map/all_to_all | solution.py:128
  (695 shorter events, 549.1 us)
Async XLA Ops:
  8.7 11.4 %copy-start.2 = (s32[4]{0:T(128)S(1)}, s32[4]{0:T(128)}, u32[]{:S(2)}) copy-start(s32[4]{0:T(128)} %param.20) | copy-start | bytes 52
  8.7 24.8 %copy-start.1 = (s32[4,128]{1,0:T(4,128)S(1)}, s32[4,128]{1,0:T(4,128)}, u32[]{:S(2)}) copy-start(s32[4,128]{1,0:T(4,128)} %param.21) | copy-start | bytes 6148
  8.7 24.9 %copy-start.3 = (f32[4,128,1,1]{1,3,2,0:T(1,128)S(1)}, f32[4,128,1,1]{1,3,2,0:T(1,128)}, u32[]{:S(2)}) copy-start(f32[4,128,1,1]{1,3,2,0:T(1,128)} %param.19) | copy-start | bytes 6148
  8.7 106.9 %all-to-all-start = ((f32[2,2048,256]{2,0,1:T(2,128)}), f32[2,2048,256]{2,0,1:T(2,128)}, u32[]{:S(2)}, u32[]{:S(2)}) async-start(f32[2,2048,256]{2,0,1:T(2,128)} %copy.26), calls=%async_computation | async-start | bytes 8388608 | tf_op jit(solution)/shard_map/all_to_all | solution.py:104
  118.5 4.4 copy-start
  122.8 88.0 %copy-start.4 = (f32[4,128]{1,0:T(4,128)S(1)}, f32[4,128]{1,0:T(4,128)}, u32[]{:S(2)}) copy-start(f32[4,128]{1,0:T(4,128)} %param.17) | copy-start | bytes 6148
  122.8 88.0 %copy-start.5 = (f32[4,128]{1,0:T(4,128)S(1)}, f32[4,128]{1,0:T(4,128)}, u32[]{:S(2)}) copy-start(f32[4,128]{1,0:T(4,128)} %param.18) | copy-start | bytes 6148
where the time goes:
time: 1140 us; the launch traced here: 1130 us
  blocking collectives  400 us (35%)
  matrix products  395 us (35%)
  other arithmetic  137 us (12%)
  local copies, waits for them, and re-layouts  90.3 us (8%)
  waiting for transfers between devices  81.9 us (7%)
  between operations  13 us (1%)
  starting transfers between devices  11.4 us (1%)
    psum x4, blocking collectives, spread_2(): return lax.psum(jnp.where(mine, shard, jnp.zeros_like(shard)), axis)  298 us
    dot_general x128, matrix products, regression(): return state_cols + jnp.dot(increment.T, gain_rows, precision=PRECISE)  226 us
    dot_general x128, matrix products, regression(): covariance = jnp.dot(anomaly, deviation, precision=PRECISE) / (members - 1)  169 us
    reduce_sum x128, other arithmetic, regression(): deviation = state_cols - jnp.mean(state_cols, axis=0, keepdims=True)  134 us
    all_to_all x1, blocking collectives, local(): lax.all_to_all(tile_state.reshape(members, tile_rows, tile_cols), 'gx', s...  103 us
    all_to_all x1, waiting for transfers between devices, local(): lax.all_to_all(ensemble, 'gx', split_axis=1, concat_axis=0, tiled=True)  81.9 us
    transpose x4, local copies, waits for them, and re-layouts, blocked_regression(): return updated.transpose(1, 0, 2).reshape(members, cell_count)  27.2 us
  transfers between devices with their start and end apart: 1, of which 1 were waited for; matrix products, arithmetic and copies ran while one was open for 0% of the time, Pallas kernels for 0%

commit v1 on v0

v1 whole, which is shorter than its diff:
```python
import functools

import jax
import jax.numpy as jnp
from jax import lax
from jax.experimental import pallas as pl
from jax.experimental.pallas import tpu as pltpu
from jax.sharding import PartitionSpec as P

MESH = pl.DeviceIdType.MESH
EPSILON = 1e-06
F32 = jnp.float32
BF16 = jnp.bfloat16
HI = lax.Precision.HIGHEST
CH = 8
GROUP = 4
PAIRS = ((0, 1, 4), (0, 2, 5), (0, 3, 6), (1, 2, 12), (1, 3, 13), (2, 3, 14))


def split(a):
    hi = a.astype(BF16)
    return hi, (a - hi.astype(F32)).astype(BF16)


def kernel(
    dims,
    owner_s,
    cells_s,
    cells_v,
    values_v,
    errors_v,
    weight_v,
    ens,
    out,
    recv,
    stage,
    pay,
    gyb,
    pay2,
    gxb,
    xobs,
    a_tab,
    i_tab,
    t_tab,
    o_tab,
    gy_s,
    gy_r,
    gx_s,
    gx_r,
    in_s,
    in_r,
    in_l,
    out_s,
    out_r,
    out_l,
):
    nx, ny, members, rows, cols, nb, nobs = dims
    chunks = rows // CH
    sides = cols // 128
    reach = float(rows * nx // 4)
    gx = lax.axis_index("gx")
    gy = lax.axis_index("gy")
    px = gx // 8
    pz = lax.rem(gx, 8)

    def partner(q):
        t = q // 4
        hop = (t + 1) // 2
        dz = jnp.where(lax.rem(t, 2) == 1, hop, 8 - hop)
        return lax.rem(px + lax.rem(q, 4), 4) * 8 + lax.rem(pz + dz, 8)

    barrier = pltpu.get_barrier_semaphore()

    def greet_x(q, c):
        pl.semaphore_signal(
            barrier, inc=1, device_id=(lax.rem(gx + q, nx), gy), device_id_type=MESH
        )
        return c

    def greet_y(q, c):
        pl.semaphore_signal(
            barrier, inc=1, device_id=(gx, lax.rem(gy + q, ny)), device_id_type=MESH
        )
        return c

    lax.fori_loop(1, ny, greet_y, 0)
    lax.fori_loop(1, nx, greet_x, 0)

    lane = lax.broadcasted_iota(jnp.int32, (nobs, 128), 1)
    cells = cells_v[...]
    cx = cells // cols
    cy = cells - cx * cols
    ox_rows, oy_rows = [], []
    for b in range(nb):
        io = owner_s[b] // ny
        jo = owner_s[b] - io * ny
        ox_rows.append((cx[b : b + 1] + io * rows).astype(F32) * (1.0 / reach))
        oy_rows.append((cy[b : b + 1] + jo * cols).astype(F32) * (1.0 / reach))
    table = jnp.concatenate(
        ox_rows + oy_rows + [(cy - cy // 128 * 128).astype(F32), jnp.zeros((nobs - 3 * nb, nobs), F32)], axis=0
    )
    table_t = table.T

    lane_pos = lane.astype(F32)
    for b in range(nb):
        base = (owner_s[b] // ny) * rows

        def fetch(k, c, b=b, base=base):
            cell = cells_s[b, k]
            row = base + cell // cols
            side = lax.rem(cell, cols) // 128
            for m in range(2):
                stage[m, pl.ds(b * nobs + k, 1), :] = ens[
                    m, row // CH, side, pl.ds(lax.rem(row, CH), 1), :
                ]
            return c

        lax.fori_loop(0, nobs, fetch, 0, unroll=8)
    picked = jnp.zeros((nobs, 128), F32)
    for b in range(nb):
        hit = lane_pos == table_t[:, 2 * nb + b : 2 * nb + b + 1]
        mine = (owner_s[b] - (owner_s[b] // ny) * ny == gy).astype(F32)
        for m in range(2):
            rows_here = stage[m, b * nobs : (b + 1) * nobs, :]
            col = jnp.sum(jnp.where(hit, rows_here, 0.0), axis=1, keepdims=True) * mine
            picked = jnp.where(lane == m * 8 + b, col, picked)
    packet = picked.T[:16]
    line = lax.broadcasted_iota(jnp.int32, (16, nobs), 0)
    for b, later, r in PAIRS:
        mine = (owner_s[later] == gx * ny + gy).astype(F32)
        packet = jnp.where(line == r, weight_v[b : b + 1, :] * mine, packet)
    pay[...] = packet
    gyb[gy] = packet

    pl.semaphore_wait(barrier, nx + ny - 2)

    def send_y(q, c):
        pltpu.make_async_remote_copy(
            src_ref=pay,
            dst_ref=gyb.at[gy],
            send_sem=gy_s,
            recv_sem=gy_r,
            device_id=(gx, lax.rem(gy + q, ny)),
            device_id_type=MESH,
        ).start()
        return c

    lax.fori_loop(1, ny, send_y, 0)

    def send_in(c, carry):
        def one(q, carry2):
            peer = partner(q)
            pltpu.make_async_remote_copy(
                src_ref=ens.at[:, peer * chunks + c],
                dst_ref=recv.at[c, pl.ds(gx * 2, 2)],
                send_sem=in_s.at[c],
                recv_sem=in_r.at[c],
                device_id=(peer, gy),
                device_id_type=MESH,
            ).start()
            return carry2

        lax.fori_loop(1, nx, one, 0)
        pltpu.make_async_copy(
            ens.at[:, gx * chunks + c],
            recv.at[c, pl.ds(gx * 2, 2)],
            in_l.at[c],
        ).start()
        return carry

    lax.fori_loop(0, 1, send_in, 0)

    pltpu.make_async_copy(gyb.at[pl.ds(0, ny - 1)], gyb.at[pl.ds(0, ny - 1)], gy_r).wait()
    pltpu.make_async_copy(gyb.at[pl.ds(0, ny - 1)], gyb.at[pl.ds(0, ny - 1)], gy_s).wait()
    packet = gyb[0]
    for j in range(1, ny):
        packet = packet + gyb[j]
    pay2[...] = packet
    gxb[pl.ds(pl.multiple_of(gx * 16, 16), 16), :] = packet

    def send_x(q, c):
        pltpu.make_async_remote_copy(
            src_ref=pay2,
            dst_ref=gxb.at[pl.ds(pl.multiple_of(gx * 16, 16), 16), :],
            send_sem=gx_s,
            recv_sem=gx_r,
            device_id=(partner(q), gy),
            device_id_type=MESH,
        ).start()
        return c

    lax.fori_loop(1, nx, send_x, 0)
    lax.fori_loop(1, chunks, send_in, 0)

    part = gxb.at[pl.ds(0, (nx - 1) * 16), :]
    pltpu.make_async_copy(part, part, gx_r).wait()
    pltpu.make_async_copy(part, part, gx_s).wait()

    for b in range(nb):
        xobs[:, b * nobs : (b + 1) * nobs] = gxb[pl.ds(b, members, stride=8), :]
    w_rows = [
        jnp.sum(gxb[pl.ds(r, nx, stride=16), :], axis=0, keepdims=True) for _, _, r in PAIRS
    ]
    w_t = jnp.concatenate(w_rows + [jnp.zeros((nobs - len(PAIRS), nobs), F32)], axis=0).T

    y_here = (
        lax.broadcasted_iota(jnp.int32, (nobs, cols), 1) + gy * cols
    ).astype(F32) * (1.0 / reach)
    for b in range(nb):
        prior = xobs[:, b * nobs : (b + 1) * nobs]
        average = jnp.mean(prior, axis=0, keepdims=True)
        anomaly = prior - average
        spread = jnp.sum(anomaly * anomaly, axis=0, keepdims=True) / (members - 1) + EPSILON
        noise = errors_v[b : b + 1, :]
        post_var = 1.0 / (1.0 / spread + 1.0 / noise)
        post_mean = post_var * (average / spread + values_v[b : b + 1, :] / noise)
        increment = post_mean - average + (jnp.sqrt(post_var / spread) - 1.0) * anomaly
        scaled = anomaly * (1.0 / ((members - 1) * spread))
        ox = table_t[:, b : b + 1]
        oy = table_t[:, nb + b : nb + b + 1]
        if b < nb - 1:
            later = xobs[:, (b + 1) * nobs :]
            deviation = later - jnp.mean(later, axis=0, keepdims=True)
            cov = jnp.dot(scaled.T, deviation, precision=HI, preferred_element_type=F32)
            gains = []
            for later_b in range(b + 1, nb):
                dx = table[later_b : later_b + 1] - ox
                dy = table[nb + later_b : nb + later_b + 1] - oy
                n = [p[:2] for p in PAIRS].index((b, later_b))
                taper = w_t[:, n : n + 1] / (1.0 + (dx * dx + dy * dy))
                at = (later_b - b - 1) * nobs
                gains.append(cov[:, at : at + nobs] * taper)
            gain = jnp.concatenate(gains, axis=1)
            xobs[:, (b + 1) * nobs :] = later + jnp.dot(
                increment, gain, precision=HI, preferred_element_type=F32
            )
        a_hi, a_lo = split((scaled * weight_v[b : b + 1, :]).T)
        a_tab[b] = jnp.concatenate([a_hi, a_lo, a_hi, a_lo], axis=1)
        i_hi, i_lo = split(increment)
        i_tab[b] = jnp.concatenate(
            [jnp.concatenate([i_hi, i_hi], axis=1), jnp.concatenate([i_lo, i_lo], axis=1)],
            axis=0,
        )
        dy = y_here - oy
        t_tab[b] = 1.0 + dy * dy
        o_tab[b] = jnp.broadcast_to(ox, (nobs, 128))

    def work(c, carry):
        some = recv.at[c, pl.ds(0, 2 * (nx - 1))]
        pltpu.make_async_copy(some, some, in_r.at[c]).wait()
        own = recv.at[c, pl.ds(gx * 2, 2)]
        pltpu.make_async_copy(own, own, in_l.at[c]).wait()
        flat = recv.at[c].reshape(members * sides * CH, 128)

        def group(g, carry2):
            first = g * GROUP
            x = jnp.concatenate(
                [
                    flat[pl.ds(first + r + h * CH, members, stride=sides * CH), :]
                    for r in range(GROUP)
                    for h in range(sides)
                ],
                axis=1,
            )
            for b in range(nb):
                deviation = x - jnp.mean(x, axis=0, keepdims=True)
                d_hi, d_lo = split(deviation)
                cov = jnp.dot(
                    a_tab[b],
                    jnp.concatenate([d_hi, d_hi, d_lo, d_lo], axis=0),
                    preferred_element_type=F32,
                )
                gains = []
                for r in range(GROUP):
                    x_here = (gx * rows + c * CH + first + r).astype(F32) * (1.0 / reach)
                    dx = x_here - o_tab[b]
                    dx = dx * dx
                    far = t_tab[b] + jnp.concatenate([dx] * sides, axis=1)
                    gains.append(cov[:, r * cols : (r + 1) * cols] / far)
                g_hi, g_lo = split(jnp.concatenate(gains, axis=1))
                change = jnp.dot(
                    i_tab[b],
                    jnp.concatenate([g_hi, g_lo], axis=0),
                    preferred_element_type=F32,
                )
                x = x + (change[:members] + change[members:])
            for r in range(GROUP):
                for h in range(sides):
                    at = r * cols + h * 128
                    flat[pl.ds(first + r + h * CH, members, stride=sides * CH), :] = x[
                        :, at : at + 128
                    ]
            return carry2

        lax.fori_loop(0, CH // GROUP, group, 0)

        there = gx * chunks + c

        def one(q, carry2):
            peer = partner(q)
            pltpu.make_async_remote_copy(
                src_ref=recv.at[c, pl.ds(peer * 2, 2)],
                dst_ref=out.at[:, there],
                send_sem=out_s.at[c],
                recv_sem=out_r,
                device_id=(peer, gy),
                device_id_type=MESH,
            ).start()
            return carry2

        lax.fori_loop(1, nx, one, 0)
        pltpu.make_async_copy(
            recv.at[c, pl.ds(gx * 2, 2)], out.at[:, there], out_l.at[c]
        ).start()
        return carry

    lax.fori_loop(0, chunks, work, 0)

    def finish(c, carry):
        some = recv.at[c, pl.ds(0, 2 * (nx - 1))]
        pltpu.make_async_copy(some, some, in_s.at[c]).wait()
        pltpu.make_async_copy(some, some, out_s.at[c]).wait()
        there = out.at[:, gx * chunks + c]
        pltpu.make_async_copy(recv.at[c, pl.ds(gx * 2, 2)], there, out_l.at[c]).wait()
        return carry

    lax.fori_loop(0, chunks, finish, 0)
    rest = out.at[:, pl.ds(0, (nx - 1) * chunks)]
    pltpu.make_async_copy(rest, rest, out_r).wait()


def local(nx, ny, ensemble, obs_values, obs_error, tile_weight, owner_device, obs_cells):
    own, length, cols = ensemble.shape
    nb, nobs = obs_cells.shape
    members = own * nx
    rows = length // nx
    chunks = rows // CH
    dims = (nx, ny, members, rows, cols, nb, nobs)
    vmem = pl.BlockSpec(memory_space=pltpu.VMEM)
    smem = pl.BlockSpec(memory_space=pltpu.SMEM)
    dma = pltpu.SemaphoreType.DMA
    tiles = ensemble.reshape(own, length // CH, CH, cols // 128, 128).transpose(0, 1, 3, 2, 4)
    result = pl.pallas_call(
        functools.partial(kernel, dims),
        out_shape=jax.ShapeDtypeStruct(tiles.shape, F32),
        in_specs=[smem, smem, vmem, vmem, vmem, vmem, vmem],
        out_specs=pl.BlockSpec(memory_space=pl.ANY),
        scratch_shapes=[
            pltpu.VMEM((chunks, members, cols // 128, CH, 128), F32),
            pltpu.VMEM((2, nb * nobs, 128), F32),
            pltpu.VMEM((16, nobs), F32),
            pltpu.VMEM((ny, 16, nobs), F32),
            pltpu.VMEM((16, nobs), F32),
            pltpu.VMEM((nx * 16, nobs), F32),
            pltpu.VMEM((members, nb * nobs), F32),
            pltpu.VMEM((nb, nobs, 4 * members), BF16),
            pltpu.VMEM((nb, 2 * members, 2 * nobs), BF16),
            pltpu.VMEM((nb, nobs, cols), F32),
            pltpu.VMEM((nb, nobs, 128), F32),
            dma,
            dma,
            dma,
            dma,
            dma((chunks,)),
            dma((chunks,)),
            dma((chunks,)),
            dma((chunks,)),
            dma,
            dma((chunks,)),
        ],
        compiler_params=pltpu.CompilerParams(
            collective_id=0, has_side_effects=True, vmem_limit_bytes=40 * 1024 * 1024
        ),
    )(
        owner_device,
        obs_cells,
        obs_cells,
        obs_values,
        obs_error,
        tile_weight.reshape(nb, nobs),
        tiles,
    )
    return result.transpose(0, 1, 3, 2, 4).reshape(ensemble.shape)


def solution(mesh):
    placed = (P("gx", None, "gy"), P(), P(), P(None, None, "gx", "gy"), P(), P())
    return jax.shard_map(
        functools.partial(local, mesh.shape["gx"], mesh.shape["gy"]),
        mesh=mesh,
        in_specs=placed,
        out_specs=P("gx", None, "gy"),
        check_vma=False,
    )
```

time: 1140 us -> 214 us (0.19)
  blocking collectives: 400 us -> 0 us
  matrix products: 395 us -> 0 us
  Pallas kernels: 0 us -> 204 us
  other arithmetic: 137 us -> 0 us
  local copies, waits for them, and re-layouts: 90.3 us -> 7.58 us
  waiting for transfers between devices: 81.9 us -> 0 us
  between operations: 13 us -> 0.02 us
  starting transfers between devices: 11.4 us -> 0 us
    dot_general x256 -> x0, matrix products: 395 us -> none  [the longest x128 226 us: regression(): return state_cols + jnp.dot(increment.T, gain_rows, precision=PRECISE)]
    psum x4 -> x0, blocking collectives: 298 us -> none  [spread_2(): return lax.psum(jnp.where(mine, shard, jnp.zeros_like(shard)), axis)]
    pallas_call x0 -> x1, Pallas kernels: none -> 204 us  [local(): pl.pallas_call(functools.partial(kernel, dims), out_shape=jax.ShapeDtypeS...]
    reduce_sum x136 -> x0, other arithmetic: 135 us -> none  [the longest x128 134 us: regression(): deviation = state_cols - jnp.mean(state_cols, axis=0, keepdims=True)]
    all_to_all x1 -> x0, blocking collectives: 103 us -> none  [local(): lax.all_to_all(tile_state.reshape(members, tile_rows, tile_cols), 'gx', s...]
    all_to_all x1 -> x0, waiting for transfers between devices: 81.9 us -> none  [local(): lax.all_to_all(ensemble, 'gx', split_axis=1, concat_axis=0, tiled=True)]
    transpose x4 -> x0, local copies, waits for them, and re-layouts: 27.2 us -> none  [blocked_regression(): return updated.transpose(1, 0, 2).reshape(members, cell_count)]
    another operation x7 -> x0, local copies, waits for them, and re-layouts: 20.2 us -> none
  transfers between devices with their start and end apart: 1 -> 0, of which waited for: 1 -> 0; matrix products, arithmetic and copies ran while one was open for 0% -> 0% of each run, Pallas kernels for 0% -> 0%
where the time goes in v1:
time: 214 us; the launch traced here: 212 us
  Pallas kernels  204 us (95%)
  local copies, waits for them, and re-layouts  7.58 us (4%)
    pallas_call x1, Pallas kernels, local(): pl.pallas_call(functools.partial(kernel, dims), out_shape=jax.ShapeDtypeS...  204 us
    unnamed x13, local copies, waits for them, and re-layouts  7.58 us

profile of v1, /device:TPU:32, one launch (start us, length us, event | category | flops | bytes accessed | tf_op | source)
XLA Modules:
  0.0 212.0 jit_solution(2234941870751220365)
XLA Ops:
  0.0 0.0 copy-start
  0.0 2.2 %copy-done = f32[2,2048,256]{2,1,0:T(8,128)S(1)} copy-done((f32[2,2048,256]{2,1,0:T(8,128)S(1)}, f32[2,2048,256]{2,1,0:T(8,128)}, u32[]{:S(2)}) %copy-start) | copy-done | bytes 4194328
  2.2 0.0 copy-start.1
  2.2 0.7 copy-done.1
  2.9 0.0 copy-start.2
  2.9 0.7 copy-done.2
  3.6 0.0 copy-start.3
  3.6 0.7 copy-done.3
  4.2 0.0 copy-start.4
  4.2 0.7 copy-done.4
  4.9 0.0 copy-start.5
  4.9 0.7 copy-done.5
  5.6 204.4 %shard_map.64 = f32[2,256,2,8,128]{4,3,2,1,0:T(8,128)S(1)} custom-call(s32[4]{0:T(128)S(1)} %copy-done.5, s32[4,128]{1,0:T(4,128)S(1)} %copy-done.1, s32[4,128]{1,0:T(4,128)S(1)} %copy-done.1, f32[4,128]{1,0:T(4,128)S(1)} %copy-done.2, f32[4,128]{1,0:T(4,128)S(1)} %copy-done.3, f32[4,128]{1,0:T(4,128)S(1)} %bitcast.9, f32[2,256,2,8,128]{4,3,2,1,0:T(8,128)S(1)} %bitcast.8), custom_call_target="tpu_custom_call" | custom-call | tf_op jit(solution)/shard_map/pallas_call | solution.py:343
  210.0 2.0 copy.8
Async XLA Ops:
  0.0 2.2 %copy-start = (f32[2,2048,256]{2,1,0:T(8,128)S(1)}, f32[2,2048,256]{2,1,0:T(8,128)}, u32[]{:S(2)}) copy-start(f32[2,2048,256]{2,1,0:T(8,128)} %param.6) | copy-start | bytes 12582916
  2.2 0.7 copy-start.1
  2.9 0.7 copy-start.2
  3.6 0.7 copy-start.3
  4.2 0.7 copy-start.4
  4.9 0.7 copy-start.5

commit v2 on v1

--- a/solution.py
+++ b/solution.py
@@ -14,7 +14,10 @@
 HI = lax.Precision.HIGHEST
 CH = 8
 GROUP = 4
-PAIRS = ((0, 1, 4), (0, 2, 5), (0, 3, 6), (1, 2, 12), (1, 3, 13), (2, 3, 14))
+EARLY = 2
+MIDDLE = 3
+LATE = 4
+PAIRS = ((0, 1), (0, 2), (0, 3), (1, 2), (1, 3), (2, 3))
 
 
 def split(a):
@@ -24,6 +27,13 @@
 
 def kernel(
     dims,
+    owner_h,
+    cells_h,
+    values_h,
+    errors_h,
+    weight_h,
+    ens_h,
+    out,
     owner_s,
     cells_s,
     cells_v,
@@ -31,12 +41,10 @@
     errors_v,
     weight_v,
     ens,
-    out,
     recv,
     stage,
     pay,
     gyb,
-    pay2,
     gxb,
     xobs,
     a_tab,
@@ -47,12 +55,15 @@
     gy_r,
     gx_s,
     gx_r,
+    all_s,
+    all_r,
     in_s,
     in_r,
     in_l,
     out_s,
     out_r,
     out_l,
+    load,
 ):
     nx, ny, members, rows, cols, nb, nobs = dims
     chunks = rows // CH
@@ -85,6 +96,47 @@
 
     lax.fori_loop(1, ny, greet_y, 0)
     lax.fori_loop(1, nx, greet_x, 0)
+
+    loads = [
+        pltpu.make_async_copy(src, dst, load.at[n])
+        for n, (src, dst) in enumerate(
+            (
+                (owner_h, owner_s),
+                (cells_h, cells_s),
+                (cells_h, cells_v),
+                (values_h, values_v),
+                (errors_h, errors_v),
+                (weight_h, weight_v),
+                (ens_h, ens),
+            )
+        )
+    ]
+    for copy in loads:
+        copy.start()
+
+    def send_in(c, carry):
+        def one(q, carry2):
+            peer = partner(q)
+            pltpu.make_async_remote_copy(
+                src_ref=ens_h.at[:, peer * chunks + c],
+                dst_ref=recv.at[c, pl.ds(gx * 2, 2)],
+                send_sem=in_s.at[c],
+                recv_sem=in_r.at[c],
+                device_id=(peer, gy),
+                device_id_type=MESH,
+            ).start()
+            return carry2
+
+        lax.fori_loop(1, nx, one, 0)
+        pltpu.make_async_copy(
+            ens_h.at[:, gx * chunks + c], recv.at[c, pl.ds(gx * 2, 2)], in_l.at[c]
+        ).start()
+        return carry
+
+    pl.semaphore_wait(barrier, nx + ny - 2)
+    lax.fori_loop(0, EARLY, send_in, 0)
+    for copy in loads:
+        copy.wait()
 
     lane = lax.broadcasted_iota(jnp.int32, (nobs, 128), 1)
     cells = cells_v[...]
@@ -123,65 +175,44 @@
         for m in range(2):
             rows_here = stage[m, b * nobs : (b + 1) * nobs, :]
             col = jnp.sum(jnp.where(hit, rows_here, 0.0), axis=1, keepdims=True) * mine
-            picked = jnp.where(lane == m * 8 + b, col, picked)
+            picked = jnp.where(lane == 2 * b + m, col, picked)
     packet = picked.T[:16]
     line = lax.broadcasted_iota(jnp.int32, (16, nobs), 0)
-    for b, later, r in PAIRS:
+    for n, (b, later) in enumerate(PAIRS):
         mine = (owner_s[later] == gx * ny + gy).astype(F32)
-        packet = jnp.where(line == r, weight_v[b : b + 1, :] * mine, packet)
+        packet = jnp.where(line == 2 * nb + n, weight_v[b : b + 1, :] * mine, packet)
     pay[...] = packet
-    gyb[gy] = packet
-
-    pl.semaphore_wait(barrier, nx + ny - 2)
+    for i in range(2):
+        gyb[pl.ds(2 * gy + i, 1), :] = pay[pl.ds(2 * gy + i, 1), :]
 
     def send_y(q, c):
+        peer = lax.rem(gy + q, ny)
         pltpu.make_async_remote_copy(
-            src_ref=pay,
-            dst_ref=gyb.at[gy],
+            src_ref=pay.at[pl.ds(2 * peer, 2), :],
+            dst_ref=gyb.at[pl.ds(2 * gy, 2), :],
             send_sem=gy_s,
             recv_sem=gy_r,
-            device_id=(gx, lax.rem(gy + q, ny)),
+            device_id=(gx, peer),
             device_id_type=MESH,
         ).start()
         return c
 
     lax.fori_loop(1, ny, send_y, 0)
-
-    def send_in(c, carry):
-        def one(q, carry2):
-            peer = partner(q)
-            pltpu.make_async_remote_copy(
-                src_ref=ens.at[:, peer * chunks + c],
-                dst_ref=recv.at[c, pl.ds(gx * 2, 2)],
-                send_sem=in_s.at[c],
-                recv_sem=in_r.at[c],
-                device_id=(peer, gy),
-                device_id_type=MESH,
-            ).start()
-            return carry2
-
-        lax.fori_loop(1, nx, one, 0)
-        pltpu.make_async_copy(
-            ens.at[:, gx * chunks + c],
-            recv.at[c, pl.ds(gx * 2, 2)],
-            in_l.at[c],
-        ).start()
-        return carry
-
-    lax.fori_loop(0, 1, send_in, 0)
-
-    pltpu.make_async_copy(gyb.at[pl.ds(0, ny - 1)], gyb.at[pl.ds(0, ny - 1)], gy_r).wait()
-    pltpu.make_async_copy(gyb.at[pl.ds(0, ny - 1)], gyb.at[pl.ds(0, ny - 1)], gy_s).wait()
-    packet = gyb[0]
-    for j in range(1, ny):
-        packet = packet + gyb[j]
-    pay2[...] = packet
-    gxb[pl.ds(pl.multiple_of(gx * 16, 16), 16), :] = packet
+    lax.fori_loop(EARLY, MIDDLE, send_in, 0)
+
+    part = gyb.at[pl.ds(0, 2 * (ny - 1)), :]
+    pltpu.make_async_copy(part, part, gy_r).wait()
+    pltpu.make_async_copy(part, part, gy_s).wait()
+    for i in range(2):
+        gxb[gy, pl.ds(2 * gx + i, 1), :] = jnp.sum(
+            gyb[pl.ds(i, ny, stride=2), :], axis=0, keepdims=True
+        )
 
     def send_x(q, c):
+        mine = gxb.at[gy, pl.ds(2 * gx, 2), :]
         pltpu.make_async_remote_copy(
-            src_ref=pay2,
-            dst_ref=gxb.at[pl.ds(pl.multiple_of(gx * 16, 16), 16), :],
+            src_ref=mine,
+            dst_ref=mine,
             send_sem=gx_s,
             recv_sem=gx_r,
             device_id=(partner(q), gy),
@@ -190,16 +221,33 @@
         return c
 
     lax.fori_loop(1, nx, send_x, 0)
-    lax.fori_loop(1, chunks, send_in, 0)
-
-    part = gxb.at[pl.ds(0, (nx - 1) * 16), :]
+    lax.fori_loop(MIDDLE, LATE, send_in, 0)
+    part = gxb.at[0, pl.ds(0, 2 * (nx - 1)), :]
     pltpu.make_async_copy(part, part, gx_r).wait()
     pltpu.make_async_copy(part, part, gx_s).wait()
 
+    def send_all(q, c):
+        pltpu.make_async_remote_copy(
+            src_ref=gxb.at[gy],
+            dst_ref=gxb.at[gy],
+            send_sem=all_s,
+            recv_sem=all_r,
+            device_id=(gx, lax.rem(gy + q, ny)),
+            device_id_type=MESH,
+        ).start()
+        return c
+
+    lax.fori_loop(1, ny, send_all, 0)
+    lax.fori_loop(LATE, chunks, send_in, 0)
+    part = gxb.at[pl.ds(0, ny - 1)]
+    pltpu.make_async_copy(part, part, all_r).wait()
+    pltpu.make_async_copy(part, part, all_s).wait()
+
     for b in range(nb):
-        xobs[:, b * nobs : (b + 1) * nobs] = gxb[pl.ds(b, members, stride=8), :]
+        xobs[:, b * nobs : (b + 1) * nobs] = gxb[b]
     w_rows = [
-        jnp.sum(gxb[pl.ds(r, nx, stride=16), :], axis=0, keepdims=True) for _, _, r in PAIRS
+        jnp.sum(gxb[nb + n // 2, pl.ds(n % 2, nx, stride=2), :], axis=0, keepdims=True)
+        for n in range(len(PAIRS))
     ]
     w_t = jnp.concatenate(w_rows + [jnp.zeros((nobs - len(PAIRS), nobs), F32)], axis=0).T
 
@@ -226,7 +274,7 @@
             for later_b in range(b + 1, nb):
                 dx = table[later_b : later_b + 1] - ox
                 dy = table[nb + later_b : nb + later_b + 1] - oy
-                n = [p[:2] for p in PAIRS].index((b, later_b))
+                n = PAIRS.index((b, later_b))
                 taper = w_t[:, n : n + 1] / (1.0 + (dx * dx + dy * dy))
                 at = (later_b - b - 1) * nobs
                 gains.append(cov[:, at : at + nobs] * taper)
@@ -336,22 +384,27 @@
     rows = length // nx
     chunks = rows // CH
     dims = (nx, ny, members, rows, cols, nb, nobs)
-    vmem = pl.BlockSpec(memory_space=pltpu.VMEM)
-    smem = pl.BlockSpec(memory_space=pltpu.SMEM)
+    hbm = pl.BlockSpec(memory_space=pltpu.HBM)
     dma = pltpu.SemaphoreType.DMA
     tiles = ensemble.reshape(own, length // CH, CH, cols // 128, 128).transpose(0, 1, 3, 2, 4)
     result = pl.pallas_call(
         functools.partial(kernel, dims),
-        out_shape=jax.ShapeDtypeStruct(tiles.shape, F32),
-        in_specs=[smem, smem, vmem, vmem, vmem, vmem, vmem],
+        out_shape=pltpu.VMEM(tiles.shape, F32),
+        in_specs=[hbm] * 6,
         out_specs=pl.BlockSpec(memory_space=pl.ANY),
         scratch_shapes=[
+            pltpu.SMEM((nb,), jnp.int32),
+            pltpu.SMEM((nb, nobs), jnp.int32),
+            pltpu.VMEM((nb, nobs), jnp.int32),
+            pltpu.VMEM((nb, nobs), F32),
+            pltpu.VMEM((nb, nobs), F32),
+            pltpu.VMEM((nb, nobs), F32),
+            pltpu.VMEM(tiles.shape, F32),
             pltpu.VMEM((chunks, members, cols // 128, CH, 128), F32),
             pltpu.VMEM((2, nb * nobs, 128), F32),
             pltpu.VMEM((16, nobs), F32),
-            pltpu.VMEM((ny, 16, nobs), F32),
-            pltpu.VMEM((16, nobs), F32),
-            pltpu.VMEM((nx * 16, nobs), F32),
+            pltpu.VMEM((2 * ny, nobs), F32),
+            pltpu.VMEM((ny, 2 * nx, nobs), F32),
             pltpu.VMEM((members, nb * nobs), F32),
             pltpu.VMEM((nb, nobs, 4 * members), BF16),
             pltpu.VMEM((nb, 2 * members, 2 * nobs), BF16),
@@ -361,19 +414,21 @@
             dma,
             dma,
             dma,
+            dma,
+            dma,
             dma((chunks,)),
             dma((chunks,)),
             dma((chunks,)),
             dma((chunks,)),
             dma,
             dma((chunks,)),
+            dma((7,)),
         ],
         compiler_params=pltpu.CompilerParams(
-            collective_id=0, has_side_effects=True, vmem_limit_bytes=40 * 1024 * 1024
+            collective_id=0, has_side_effects=True, vmem_limit_bytes=52 * 1024 * 1024
         ),
     )(
         owner_device,
-        obs_cells,
         obs_cells,
         obs_values,
         obs_error,

time: 214 us -> 196 us (0.916)
  Pallas kernels: 204 us -> 194 us
  local copies, waits for them, and re-layouts: 7.58 us -> 2.02 us
    pallas_call x1, Pallas kernels: 204 us -> 194 us  [local(): pl.pallas_call(functools.partial(kernel, dims), out_shape=pltpu.VMEM(tile...]
    unnamed x13 -> x1, local copies, waits for them, and re-layouts: 7.58 us -> 2.02 us
where the time goes in v2:
time: 196 us
  Pallas kernels  194 us (99%)
  local copies, waits for them, and re-layouts  2.02 us (1%)
    pallas_call x1, Pallas kernels, local(): pl.pallas_call(functools.partial(kernel, dims), out_shape=pltpu.VMEM(tile...  194 us

profile of v2, /device:TPU:32, one launch (start us, length us, event | category | flops | bytes accessed | tf_op | source)
XLA Modules:
  0.0 196.0 jit_solution(1131415938671786372)
XLA Ops:
  0.0 193.9 %shard_map.64 = f32[2,256,2,8,128]{4,3,2,1,0:T(8,128)S(1)} custom-call(s32[4]{0:T(128)} %owner_h.1, s32[4,128]{1,0:T(4,128)} %cells_h.1, f32[4,128]{1,0:T(4,128)} %values_h.1, f32[4,128]{1,0:T(4,128)} %errors_h.1, f32[4,128]{1,0:T(4,128)} %bitcast.9, f32[2,256,2,8,128]{4,3,2,1,0:T(8,128)} %bitcast.8), custom_call_target="tpu_custom_call" | custom-call | tf_op jit(solution)/shard_map/pallas_call | solution.py:390
  193.9 2.0 %copy.8 = f32[2,2048,256]{2,1,0:T(8,128)} copy(f32[2,2048,256]{2,1,0:T(8,128)S(1)} %bitcast.7) | data formatting | bytes 8388608

commit v3 on v2

--- a/solution.py
+++ b/solution.py
@@ -64,6 +64,8 @@
     out_r,
     out_l,
     load,
+    gate_sem,
+    open_sem,
 ):
     nx, ny, members, rows, cols, nb, nobs = dims
     chunks = rows // CH
@@ -94,8 +96,12 @@
         )
         return c
 
-    lax.fori_loop(1, ny, greet_y, 0)
+    gate = nx - 1
     lax.fori_loop(1, nx, greet_x, 0)
+
+    @pl.when(gx == gate)
+    def _():
+        lax.fori_loop(1, ny, greet_y, 0)
 
     loads = [
         pltpu.make_async_copy(src, dst, load.at[n])
@@ -133,8 +139,34 @@
         ).start()
         return carry
 
-    pl.semaphore_wait(barrier, nx + ny - 2)
+    def plane_ready(q, c):
+        pl.semaphore_signal(
+            gate_sem, inc=1, device_id=(gx, lax.rem(gy + q, ny)), device_id_type=MESH
+        )
+        return c
+
+    def all_ready(q, c):
+        pl.semaphore_signal(
+            open_sem, inc=1, device_id=(lax.rem(gx + q, nx), gy), device_id_type=MESH
+        )
+        return c
+
+    @pl.when(gx != gate)
+    def _():
+        pl.semaphore_wait(barrier, nx - 1)
+
+    @pl.when(gx == gate)
+    def _():
+        pl.semaphore_wait(barrier, nx + ny - 2)
+        lax.fori_loop(1, ny, plane_ready, 0)
+
     lax.fori_loop(0, EARLY, send_in, 0)
+
+    @pl.when(gx == gate)
+    def _():
+        pl.semaphore_wait(gate_sem, ny - 1)
+        lax.fori_loop(1, nx, all_ready, 0)
+
     for copy in loads:
         copy.wait()
 
@@ -184,6 +216,10 @@
     pay[...] = packet
     for i in range(2):
         gyb[pl.ds(2 * gy + i, 1), :] = pay[pl.ds(2 * gy + i, 1), :]
+
+    @pl.when(gx != gate)
+    def _():
+        pl.semaphore_wait(open_sem, 1)
 
     def send_y(q, c):
         peer = lax.rem(gy + q, ny)
@@ -423,6 +459,8 @@
             dma,
             dma((chunks,)),
             dma((7,)),
+            pltpu.SemaphoreType.REGULAR,
+            pltpu.SemaphoreType.REGULAR,
         ],
         compiler_params=pltpu.CompilerParams(
             collective_id=0, has_side_effects=True, vmem_limit_bytes=52 * 1024 * 1024

time: 196 us -> 195 us (level)
  Pallas kernels: 194 us -> 192 us
where the time goes in v3:
time: 195 us; the launch traced here: 194 us
  Pallas kernels  192 us (98%)
  local copies, waits for them, and re-layouts  2.02 us (1%)
    pallas_call x1, Pallas kernels, local(): pl.pallas_call(functools.partial(kernel, dims), out_shape=pltpu.VMEM(tile...  192 us

profile of v3, /device:TPU:32, one launch (start us, length us, event | category | flops | bytes accessed | tf_op | source)
XLA Modules:
  0.0 194.5 jit_solution(6393789871168073473)
XLA Ops:
  0.0 192.5 %shard_map.64 = f32[2,256,2,8,128]{4,3,2,1,0:T(8,128)S(1)} custom-call(s32[4]{0:T(128)} %owner_h.1, s32[4,128]{1,0:T(4,128)} %cells_h.1, f32[4,128]{1,0:T(4,128)} %values_h.1, f32[4,128]{1,0:T(4,128)} %errors_h.1, f32[4,128]{1,0:T(4,128)} %bitcast.9, f32[2,256,2,8,128]{4,3,2,1,0:T(8,128)} %bitcast.8), custom_call_target="tpu_custom_call" | custom-call | tf_op jit(solution)/shard_map/pallas_call | solution.py:426
  192.5 2.0 %copy.8 = f32[2,2048,256]{2,1,0:T(8,128)} copy(f32[2,2048,256]{2,1,0:T(8,128)S(1)} %bitcast.7) | data formatting | bytes 8388608

commit v4 on v3

--- a/solution.py
+++ b/solution.py
@@ -17,6 +17,7 @@
 EARLY = 2
 MIDDLE = 3
 LATE = 4
+LAST = 2
 PAIRS = ((0, 1), (0, 2), (0, 3), (1, 2), (1, 3), (2, 3))
 
 
@@ -380,8 +381,7 @@
 
         there = gx * chunks + c
 
-        def one(q, carry2):
-            peer = partner(q)
+        def send_out(peer):
             pltpu.make_async_remote_copy(
                 src_ref=recv.at[c, pl.ds(peer * 2, 2)],
                 dst_ref=out.at[:, there],
@@ -390,9 +390,20 @@
                 device_id=(peer, gy),
                 device_id_type=MESH,
             ).start()
+
+        def one(q, carry2):
+            t = q // 4
+            z_there = t // 4 * 4 + lax.rem(t + pz, 4)
+            by_half = lax.rem(px + lax.rem(q, 4), 4) * 8 + z_there
+            peer = jnp.where(c < chunks - LAST, partner(q), by_half)
+
+            @pl.when(peer != gx)
+            def _():
+                send_out(peer)
+
             return carry2
 
-        lax.fori_loop(1, nx, one, 0)
+        lax.fori_loop(0, nx, one, 0)
         pltpu.make_async_copy(
             recv.at[c, pl.ds(gx * 2, 2)], out.at[:, there], out_l.at[c]
         ).start()

time: 195 us -> 194 us (level)
  no operation moved by 1% of the time
where the time goes in v4:
time: 194 us; the launch traced here: 193 us
  Pallas kernels  191 us (98%)
  local copies, waits for them, and re-layouts  2.02 us (1%)
    pallas_call x1, Pallas kernels, local(): pl.pallas_call(functools.partial(kernel, dims), out_shape=pltpu.VMEM(tile...  191 us

profile of v4, /device:TPU:32, one launch (start us, length us, event | category | flops | bytes accessed | tf_op | source)
XLA Modules:
  0.0 193.3 jit_solution(5401265477892891972)
XLA Ops:
  0.0 191.3 %shard_map.64 = f32[2,256,2,8,128]{4,3,2,1,0:T(8,128)S(1)} custom-call(s32[4]{0:T(128)} %owner_h.1, s32[4,128]{1,0:T(4,128)} %cells_h.1, f32[4,128]{1,0:T(4,128)} %values_h.1, f32[4,128]{1,0:T(4,128)} %errors_h.1, f32[4,128]{1,0:T(4,128)} %bitcast.9, f32[2,256,2,8,128]{4,3,2,1,0:T(8,128)} %bitcast.8), custom_call_target="tpu_custom_call" | custom-call | tf_op jit(solution)/shard_map/pallas_call | solution.py:437
  191.3 2.0 %copy.8 = f32[2,2048,256]{2,1,0:T(8,128)} copy(f32[2,2048,256]{2,1,0:T(8,128)S(1)} %bitcast.7) | data formatting | bytes 8388608

commit v5 on v3

--- a/solution.py
+++ b/solution.py
@@ -97,7 +97,7 @@
         return c
 
     gate = nx - 1
-    lax.fori_loop(1, nx, greet_x, 0)
+    lax.fori_loop(1, nx, greet_x, 0, unroll=True)
 
     @pl.when(gx == gate)
     def _():

time: 195 us -> 194 us (level)
  no operation moved by 1% of the time
where the time goes in v5:
time: 194 us
  Pallas kernels  192 us (99%)
  local copies, waits for them, and re-layouts  2.02 us (1%)
    pallas_call x1, Pallas kernels, local(): pl.pallas_call(functools.partial(kernel, dims), out_shape=pltpu.VMEM(tile...  192 us

profile of v5, /device:TPU:32, one launch (start us, length us, event | category | flops | bytes accessed | tf_op | source)
XLA Modules:
  0.0 194.4 jit_solution(10704995448907097869)
XLA Ops:
  0.0 192.4 %shard_map.64 = f32[2,256,2,8,128]{4,3,2,1,0:T(8,128)S(1)} custom-call(s32[4]{0:T(128)} %owner_h.1, s32[4,128]{1,0:T(4,128)} %cells_h.1, f32[4,128]{1,0:T(4,128)} %values_h.1, f32[4,128]{1,0:T(4,128)} %errors_h.1, f32[4,128]{1,0:T(4,128)} %bitcast.9, f32[2,256,2,8,128]{4,3,2,1,0:T(8,128)} %bitcast.8), custom_call_target="tpu_custom_call" | custom-call | tf_op jit(solution)/shard_map/pallas_call | solution.py:426
  192.4 2.0 %copy.8 = f32[2,2048,256]{2,1,0:T(8,128)} copy(f32[2,2048,256]{2,1,0:T(8,128)S(1)} %bitcast.7) | data formatting | bytes 8388608
